TPU v7x, 512 devices: a whole 4x4x16 slice. The times are simulated.
512 devices in a mesh: dp: 16 (over x, y), tensor: 32 (over z, core).
Axes of the slice: x: 4, y: 4, z: 16, core: 2. Of those that a mesh axis runs over, the one named last changes fastest.
Arguments:
- mantissa: bfloat16 [1024, 4096], P('tensor', 'dp'), may hold values from -6 to 6
- block_exponents: int32 [1024, 256], P('tensor'), may hold values from -2 to 3
- norm_gain: bfloat16 [4096], P('dp'), may hold values from 0.099609375 to 1.8984375
- gate_weight: bfloat16 [4096, 14336], P('dp', 'tensor'), may hold values from -0.09375 to 0.09375
- up_weight: bfloat16 [4096, 14336], P('dp', 'tensor'), may hold values from -0.09375 to 0.09375
- down_weight: bfloat16 [14336, 4096], P('tensor', 'dp'), may hold values from -0.046875 to 0.046875
- cotangent: bfloat16 [1024, 4096], P('tensor', 'dp'), may hold values from -6 to 6
Outputs:
- mlp_output: bfloat16 [1024, 4096], P('tensor', 'dp')
- input_grad: bfloat16 [1024, 4096], P('tensor', 'dp')
- grad_gate: float32 [4096, 14336], P('dp', 'tensor')
- grad_up: float32 [4096, 14336], P('dp', 'tensor')
- grad_down: float32 [14336, 4096], P('tensor', 'dp')
All inputs are finite; a program needn't handle non-finite values.
Results may differ from a plain program's by a relative error of at most 0.04.
Values may be sent and summed in bfloat16 or wider, within the bound.
A program may use at most 64 MiB of HBM per device.

v0:
```python
import jax
import jax.numpy as jnp
from jax import lax
from jax.sharding import PartitionSpec as P

BLOCK = 16


epsilon = 1e-05


def power_of_two(exponents):
    scales = jnp.zeros(exponents.shape, jnp.float32)
    for power_level in range(-2, 4):
        scales = scales + jnp.where(exponents == power_level, 2.0**power_level, 0.0).astype(
            jnp.float32
        )
    return scales


def contract_rows(left_rows, right_rows):
    return lax.dot_general(
        left_rows, right_rows, (((1,), (1,)), ((), ())), preferred_element_type=jnp.float32
    )


def contract_tokens(left_rows, right_rows):
    return lax.dot_general(
        left_rows, right_rows, (((0,), (0,)), ((), ())), preferred_element_type=jnp.float32
    )


def shards(mantissa, block_exponents, norm_gain, gate_weight, up_weight, down_weight, cotangent):
    shard_width = gate_weight.shape[0]
    hidden_units = gate_weight.shape[1]
    full_width = block_exponents.shape[1] * BLOCK
    offset = lax.axis_index("dp") * shard_width
    expanded = jnp.repeat(block_exponents, BLOCK, axis=1)
    local_exponents = lax.dynamic_slice_in_dim(expanded, offset, shard_width, 1)
    values = mantissa.astype(jnp.float32) * power_of_two(local_exponents)
    squares = lax.psum(jnp.sum(values * values, axis=1), "dp")
    normed = (
        values * lax.rsqrt(squares[:, None] / full_width + epsilon) * norm_gain.astype(jnp.float32)
    ).astype(jnp.bfloat16)
    joined = jnp.concatenate([gate_weight, up_weight], axis=1)
    rows_all = lax.all_gather(normed, "tensor", axis=0, tiled=True)
    partial_value = jnp.dot(rows_all, joined, preferred_element_type=jnp.float32)
    summed = lax.psum(partial_value.astype(jnp.bfloat16), "dp").astype(jnp.float32)
    gate_value = summed[:, :hidden_units]
    up_value = summed[:, hidden_units:]
    logistic = jax.nn.sigmoid(gate_value)
    hidden = (gate_value * logistic * up_value).astype(jnp.bfloat16)
    row_block = hidden
    mlp_output = lax.psum_scatter(
        jnp.dot(row_block, down_weight, preferred_element_type=jnp.float32).astype(jnp.bfloat16),
        "tensor",
        scatter_dimension=0,
        tiled=True,
    )
    cot_all = lax.all_gather(cotangent, "tensor", axis=0, tiled=True)
    back_partial = contract_rows(cot_all, down_weight)
    back_sum = lax.psum(back_partial.astype(jnp.bfloat16), "dp").astype(jnp.float32)
    dgate = (back_sum * up_value * logistic * (1.0 + gate_value * (1.0 - logistic))).astype(
        jnp.bfloat16
    )
    dup_value = (back_sum * gate_value * logistic).astype(jnp.bfloat16)
    grad_hidden = jnp.concatenate([dgate, dup_value], axis=1)
    row_block = grad_hidden
    input_grad = lax.psum_scatter(
        contract_rows(row_block, joined).astype(jnp.bfloat16),
        "tensor",
        scatter_dimension=0,
        tiled=True,
    )
    grad_joined = contract_tokens(rows_all, grad_hidden)
    grad_gate = grad_joined[:, :hidden_units]
    grad_up = grad_joined[:, hidden_units:]
    grad_down = contract_tokens(hidden, cot_all)
    return (mlp_output, input_grad, grad_gate, grad_up, grad_down)


def solution(mesh):
    in_specs = (
        P("tensor", "dp"),
        P("tensor", None),
        P("dp"),
        P("dp", "tensor"),
        P("dp", "tensor"),
        P("tensor", "dp"),
        P("tensor", "dp"),
    )
    out_specs = (
        P("tensor", "dp"),
        P("tensor", "dp"),
        P("dp", "tensor"),
        P("dp", "tensor"),
        P("tensor", "dp"),
    )
    return jax.shard_map(shards, mesh=mesh, in_specs=in_specs, out_specs=out_specs, check_vma=False)
```

profile of v0, /device:TPU:6, one launch (start us, length us, event | category | flops | bytes accessed | tf_op | source)
XLA Modules:
  0.0 466.5 jit_solution(5635123020013709134)
XLA Ops:
  7.2 0.0 copy-start
  7.2 0.0 all-reduce.3.cloned.1.call-start
  7.2 0.7 convert_element_type.37
  7.9 0.9 copy.26
  8.8 1.0 constant_dynamic-update-slice_fusion.1
  9.8 38.0 %all_gather.7 = bf16[1024,256]{1,0:T(8,128)(2,1)S(1)} all-gather(bf16[32,256]{1,0:T(8,128)(2,1)} %param.13), channel_id=1, replica_groups=mesh['dp'=16,'tensor'=32] {'tensor'}, dimensions={0}, use_global_device_ids=true | all-gather | bytes 540672 | tf_op jit(solution)/shard_map/all_gather | solution.py:60
  47.8 0.1 broadcast_in_dim.33
  48.0 0.1 copy.32
  48.1 0.1 multiply_reduce_fusion
  48.2 33.9 %psum.21 = f32[32]{0:T(128)S(1)} all-reduce(f32[32]{0:T(128)S(1)} %get-tuple-element.27), channel_id=1, replica_groups=mesh['dp'=16,'tensor'=32] {'dp'}, use_global_device_ids=true, to_apply=%region_1.2 | all-reduce | flops 32 | bytes 256 | tf_op jit(solution)/shard_map/psum | solution.py:41
  82.1 0.1 multiply_convert_fusion.1
  82.2 28.2 %all_gather.6 = bf16[1024,256]{1,0:T(8,128)(2,1)S(1)} all-gather(bf16[32,256]{1,0:T(8,128)(2,1)S(1)} %multiply_convert_fusion.1), channel_id=1, replica_groups=mesh['dp'=16,'tensor'=32] {'tensor'}, dimensions={0}, use_global_device_ids=true | all-gather | bytes 540672 | tf_op jit(solution)/shard_map/all_gather | solution.py:46
  110.4 1.4 convolution_convert_fusion.1
  111.8 1.9 convolution_convert_fusion
  113.7 0.0 all-reduce.3.cloned.1.call-update
  113.7 0.0 reduce-scatter.5.cloned.1.call-start
  113.8 122.5 %all-reduce.3.cloned.1.call-done = (bf16[1024,896]{0,1:T(8,128)(2,1)}, bf16[1024,448]{0,1:T(8,128)(2,1)}) async-done(((bf16[1024,896]{0,1:T(8,128)(2,1)}, bf16[1024,448]{0,1:T(8,128)(2,1)}), (bf16[1024,896]{0,1:T(8,128)(2,1)}, bf16[1024,448]{0,1:T(8,128)(2,1)})) %all-reduce.3.cloned.1.call-update) | async-done | bytes 2752528 | tf_op jit(solution)/shard_map/psum | solution.py:48
  236.2 2.0 convert_element_type.40
  238.2 2.0 fusion.2
  240.3 1.0 copy-done.1
  241.2 2.7 convolution_convert_fusion.3
  244.0 0.0 reduce-scatter.5.cloned.1.call-update
  244.0 0.0 reduce-scatter.3.cloned.1.call-start
  244.0 1.3 convolution_convert_fusion.2
  245.4 0.0 reduce-scatter.3.cloned.1.call-update
  245.4 1.9 fusion.5
  247.3 0.2 fusion.8
  247.5 1.0 copy.30
  248.5 1.0 copy.29
  249.5 1.2 fusion.9
  250.6 100.5 %reduce-scatter.5.cloned.1.call-done = bf16[32,256]{1,0:T(8,128)(2,1)} async-done(((bf16[1024,256]{1,0:T(8,128)(2,1)}), bf16[32,256]{1,0:T(8,128)(2,1)}) %reduce-scatter.5.cloned.1.call-update) | async-done | bytes 16400 | tf_op jit(solution)/shard_map/reduce_scatter | solution.py:69
  351.2 108.8 %reduce-scatter.3.cloned.1.call-done = bf16[32,256]{1,0:T(8,128)(2,1)} async-done(((bf16[1024,256]{1,0:T(8,128)(2,1)}), bf16[32,256]{1,0:T(8,128)(2,1)}) %reduce-scatter.3.cloned.1.call-update) | async-done | bytes 16400 | tf_op jit(solution)/shard_map/reduce_scatter | solution.py:54
  (13 shorter events, 0.1 us)
Async XLA Ops:
  7.2 103.2 %copy-start = (bf16[448,256]{1,0:T(8,128)(2,1)S(1)}, bf16[448,256]{1,0:T(8,128)(2,1)}, u32[]{:S(2)}) copy-start(bf16[448,256]{1,0:T(8,128)(2,1)} %param.12) | copy-start | bytes 688132
  7.2 229.1 %all-reduce.3.cloned.1.call-start = ((), (), s32[]{:S(2)}) async-start(), calls=%async_computation.4 | async-start | bytes 5505024 | tf_op jit(solution)/shard_map/psum | solution.py:48
  8.8 39.3 %copy-start.5 = (bf16[32,256]{1,0:T(8,128)(2,1)S(1)}, bf16[32,256]{1,0:T(8,128)(2,1)}, u32[]{:S(2)}) copy-start(bf16[32,256]{1,0:T(8,128)(2,1)} %param.7) | copy-start | bytes 49156
  9.8 100.6 %copy-start.4 = (bf16[256,448]{0,1:T(8,128)(2,1)S(1)}, bf16[256,448]{0,1:T(8,128)(2,1)}, u32[]{:S(2)}) copy-start(bf16[256,448]{0,1:T(8,128)(2,1)} %param.11) | copy-start | bytes 688132
  113.7 237.5 %reduce-scatter.5.cloned.1.call-start = ((), (), s32[]{:S(2)}) async-start(), calls=%async_computation.3 | async-start | bytes 540672 | tf_op jit(solution)/shard_map/reduce_scatter | solution.py:69
  236.2 2.0 copy-start.3
  240.3 1.0 copy-start.1
  243.9 1.4 copy-start.2
  244.0 216.0 %reduce-scatter.3.cloned.1.call-start = ((), (), s32[]{:S(2)}) async-start(), calls=%async_computation.2 | async-start | bytes 540672 | tf_op jit(solution)/shard_map/reduce_scatter | solution.py:54
Sparse Core Ops, SparseCore 0:
  113.8 122.3 all-reduce.2
  244.1 107.0 reduce-scatter.4
  354.8 105.1 reduce-scatter.2
where the time goes:
time: 467 us; the launch traced here: 466 us
  waiting for transfers between devices  332 us (71%)
  blocking collectives  100 us (21%)
  between operations  13.8 us (3%)
  matrix products  10.4 us (2%)
  local copies, waits for them, and re-layouts  5.15 us (1%)
  other arithmetic  4.93 us (1%)
    psum x1, waiting for transfers between devices, shards(): lax.psum(partial_value.astype(jnp.bfloat16), 'dp').astype(jnp.float32)  122 us
    reduce_scatter x1, waiting for transfers between devices, shards(): lax.psum_scatter(jnp.dot(row_block, down_weight, preferred_element_type=j...  109 us
    reduce_scatter x1, waiting for transfers between devices, shards(): lax.psum_scatter(contract_rows(row_block, joined).astype(jnp.bfloat16), '...  101 us
    all_gather x1, blocking collectives, shards(): cot_all = lax.all_gather(cotangent, 'tensor', axis=0, tiled=True)  38 us
    psum x1, blocking collectives, shards(): squares = lax.psum(jnp.sum(values * values, axis=1), 'dp')  33.9 us
    all_gather x1, blocking collectives, shards(): rows_all = lax.all_gather(normed, 'tensor', axis=0, tiled=True)  28.2 us
  transfers between devices with their start and end apart: 3, of which 3 were waited for; matrix products, arithmetic and copies ran while one was open for 1% of the time, Pallas kernels for 0%

commit v1 on v0

v1 whole, which is shorter than its diff:
```python
import jax
import jax.numpy as jnp
from jax import lax
from jax.experimental import pallas as pl
from jax.experimental.pallas import tpu as pltpu
from jax.sharding import PartitionSpec as P

BLOCK = 16
EPSILON = 1e-05
FULL_WIDTH = 4096
MESH = pl.DeviceIdType.MESH
F32, BF16 = jnp.float32, jnp.bfloat16

NX, NY, NZ = 4, 4, 16
HID = 448
WID = 256
COLS = 1408
BACK = 2 * HID
SPANS = ((0, 640), (640, 1408))

CHUNKS = ((0, 1, -1, 2), (-2, 3, -3, 4), (-4, 5, -5, 6), (-6, 7, -7, 8))
SLOT = {d: (k, p) for k, ds in enumerate(CHUNKS) for p, d in enumerate(ds)}
DIRECT = (5,)
SCHEDULE = (
    "X-1 X1 X-2 X2",
    "A0 X3 X-3 X-4",
    "X4 A1 X5 X-5",
    "B000 B001 B010 B011",
    "X6 X-6 B100 B101",
    "B110 B111 A2 X7",
    "X-7 C01 C00 X8",
    "C10 C11 A3 B200",
    "B201 B210 B211 D0",
    "D1 B300 B301 B310",
    "B311 C21 C20 E00",
    "E01 E11 E10 C30",
    "C31 D2 F000 F001",
    "F010 F011 F100 F101",
    "F110 F111 D3 E20",
    "E21 G0 R0 G1",
    "R1 I0 E30 F200",
    "F201 F210 F211 I1",
    "E31 F300 F301 J3",
    "F310 F311 G2 R2",
    "I2 G3 J1 R3",
    "I3 J-7 J-3 J7",
    "J-5 J-1 J5",
)


def dot(a, b, dims):
    return lax.dot_general(a, b, (dims, ((), ())), preferred_element_type=F32)


def rounded(total):
    tail = total[:, -128:]
    lane = lax.broadcasted_iota(jnp.int32, tail.shape, 1)
    lost = pltpu.roll(tail - tail.astype(BF16).astype(F32), 1, 1)
    tail = tail + jnp.where(lane == 65, lost, 0.0)
    return jnp.concatenate([total[:, :-128], tail], axis=1).astype(BF16)


def layer(
    m_hbm, e_hbm, g_ref, wg_hbm, wu_hbm, wd_hbm, c_hbm,
    acts_ref, joined_ref, down_ref,
    MV, EV, X, WJ, WD, PB, R1A, R1B, R2A, R2B, H, Q, E, S, LAND, ss, rs, ls,
):
    dp, tn = lax.axis_index("dp"), lax.axis_index("tensor")
    x, y = dp // NY, lax.rem(dp, NY)
    z, core = tn // 2, lax.rem(tn, 2)
    R1, R2 = (R1A, R1B), (R2A, R2B)

    def at(dx=0, dy=0, dz=0, dc=0):
        px, py = lax.rem(x + dx + NX, NX), lax.rem(y + dy + NY, NY)
        pz, pc = lax.rem(z + dz + NZ, NZ), lax.rem(core + dc, 2)
        return (px * NY + py, pz * 2 + pc)

    def on(axis, d):
        return at(dx=d) if axis == "x" else at(dy=d)

    counter = [0]
    pending = []

    def send(src, dst, device):
        n = counter[0]
        counter[0] += 1
        copy = pltpu.make_async_remote_copy(
            src_ref=src, dst_ref=dst, send_sem=ss.at[n], recv_sem=rs.at[n], device_id=device, device_id_type=MESH
        )
        copy.start()
        pending.append(copy)
        return copy

    barrier = pltpu.get_barrier_semaphore()
    near = [at(dc=1)] + [at(dz=d) for d in (1, 2, -1, -2)]
    near += [at(dx=d) for d in (1, 2, 3)] + [at(dy=d) for d in (1, 2, 3)]
    for device in near:
        pl.semaphore_signal(barrier, inc=1, device_id=device, device_id_type=MESH)

    own = X.at[SLOT[0][0], SLOT[0][1], 0]
    fetch = [
        pltpu.make_async_copy(src, dst, ls.at[i])
        for i, (src, dst) in enumerate((
            (m_hbm, MV),
            (e_hbm, EV),
            (c_hbm, own.at[:, pl.ds(WID, WID)]),
            (wg_hbm, WJ.at[pl.ds(0, HID)]),
            (wu_hbm, WJ.at[pl.ds(HID, HID)]),
            (wd_hbm, WD.at[pl.ds(0, HID)]),
        ))
    ]
    for copy in fetch:
        copy.start()
    row = lax.broadcasted_iota(jnp.int32, (WID, WID), 0)
    col = lax.broadcasted_iota(jnp.int32, (WID, WID), 1)
    pick = jnp.where(row == dp * (WID // BLOCK) + col // BLOCK, 1.0, 0.0).astype(BF16)
    WD[HID:] = jnp.zeros((64, WID), BF16)

    for copy in fetch[:3]:
        copy.wait()
    exponents = EV[...]
    scales = jnp.zeros(exponents.shape, F32)
    for level in range(-2, 4):
        scales = scales + jnp.where(exponents == level, 2.0**level, 0.0)
    scales = dot(scales.astype(BF16), pick, ((1,), (0,)))
    own[:, :WID] = (MV[...].astype(F32) * scales).astype(BF16)

    pl.semaphore_wait(barrier, len(near))

    ring = {}
    twin = {}

    def xat(d, who):
        return X.at[SLOT[d][0], SLOT[d][1], who]

    def f_pass(d):
        if d != 0:
            ring[d].wait_recv()
        for step in (-1, 1, -2, 2) if d == 0 else (-2,) if d < 0 else (2,):
            if -8 < d + step < 9:
                ring[d + step] = send(xat(d, 0), xat(d + step, 0), at(dz=-step))
        twin[d] = send(xat(d, 0), xat(d, 1), at(dc=1))

    def gain():
        return g_ref[...].astype(F32).reshape(1, WID)

    first, direct, second, gather2, gather1, forward = {}, {}, {}, {}, {}, {}
    swap, even, odd, last = {}, {}, {}, []

    def axes(k, h):
        return ("x", "y", x, y) if (k + h) % 2 == 0 else ("y", "x", y, x)

    def columns(h):
        return slice(*SPANS[h])

    def spot(k, h, index, half):
        two = pl.ds(2 * half, 2)
        return (k, index, two) if axes(k, h)[0] == "x" else (k, two, index)

    def piece(ref, k, h, index, half):
        a, b, c = spot(k, h, index, half)
        return ref.at[a, b, c, :, pl.ds(SPANS[h][0], SPANS[h][1] - SPANS[h][0])]

    def f_partial(k):
        for d in CHUNKS[k]:
            twin[d].wait_recv()
        both = X[k].reshape(256, 2 * WID)
        values = both[:, :WID].astype(F32)
        squares = jnp.sum(values * values, axis=1, keepdims=True)
        scaled = (values * gain()).astype(BF16)
        joined = dot(scaled, WJ[...], ((1,), (1,)))
        PB[k, :, :, :, :BACK] = joined.astype(BF16).reshape(4, 4, 16, BACK)
        back = dot(both[:, WID:], WD[...], ((1,), (1,)))
        lane = lax.broadcasted_iota(jnp.int32, back.shape, 1)
        high = squares.astype(BF16).astype(F32)
        back = jnp.where(lane == HID, high, jnp.where(lane == HID + 1, squares - high, back))
        PB[k, :, :, :, BACK:] = back.astype(BF16).reshape(4, 4, 16, 512)
        for h in range(2):
            a, b, ia, ib = axes(k, h)
            far = lax.rem(ia + 2, 4)
            first[k, h] = (
                send(piece(PB, k, h, far, 0), R1[h].at[k, 0], on(a, 1)),
                send(piece(PB, k, h, far, 1), R1[h].at[k, 1], on(a, -1)),
            )
        for h in range(2):
            a, b, ia, ib = axes(k, h)
            right, left = lax.rem(ia + 1, 4), lax.rem(ia + 3, 4)
            direct[k, h] = [
                send(piece(PB, k, h, right, 1), R1[h].at[k, 2], on(a, 1)),
                send(piece(PB, k, h, left, 0), R1[h].at[k, 3], on(a, -1)),
            ]

    def add_up(k, h, index, half, parts):
        a, b, c = spot(k, h, index, half)
        width = SPANS[h][1] - SPANS[h][0]
        total = PB[a, b, c, :, columns(h)].astype(F32)
        for part in parts:
            total = total + R1[h][k, part].astype(F32)
        total = total.reshape(32, width)
        total = rounded(total) if h == 1 else total.astype(BF16)
        PB[a, b, c, :, columns(h)] = total.reshape(2, 16, width)

    def f_merge(k, h, side):
        a, b, ia, ib = axes(k, h)
        to = lax.rem(ia + (1, 3)[side], 4)
        first[k, h][side].wait_recv()
        add_up(k, h, to, side, (side,))
        direct[k, h].append(send(piece(PB, k, h, to, side), R1[h].at[k, 4 + side], on(a, (1, -1)[side])))

    def f_second(k, h):
        a, b, ia, ib = axes(k, h)
        for copy in direct[k, h]:
            copy.wait_recv()
        add_up(k, h, ia, 0, (4, 3))
        add_up(k, h, ia, 1, (2, 5))
        second[k, h] = []
        for d in (2, 1, 3):
            to = lax.rem(ib + d, 4)
            px, py = (ia, to) if a == "x" else (to, ia)
            src = PB.at[k, px, py, :, pl.ds(SPANS[h][0], SPANS[h][1] - SPANS[h][0])]
            second[k, h].append(send(src, R2[h].at[k, d - 1], on(b, d)))

    def f_act(k):
        halves = []
        for h in range(2):
            for copy in second[k, h]:
                copy.wait_recv()
            total = PB[k, x, y, :, columns(h)].astype(F32)
            for part in range(3):
                total = total + R2[h][k, part].astype(F32)
            halves.append(total)
        total = jnp.concatenate(halves, axis=1)
        squares = total[:, 3 * HID : 3 * HID + 1] + total[:, 3 * HID + 1 : 3 * HID + 2]
        inv = lax.rsqrt(squares / FULL_WIDTH + EPSILON)
        gate = total[:, :HID] * inv
        up = total[:, HID : 2 * HID] * inv
        back = total[:, BACK : BACK + HID]
        sig = jax.nn.sigmoid(gate)
        hidden = gate * sig * up
        dgate = back * up * sig * (1.0 + gate * (1.0 - sig))
        dup = back * gate * sig
        high = inv.astype(BF16).astype(F32)
        lane = lax.broadcasted_iota(jnp.int32, (16, 64), 1)
        tail = jnp.where(lane == 0, high, jnp.where(lane == 1, inv - high, 0.0))
        H[k, x, y] = jnp.concatenate([dgate, dup, hidden, tail], axis=1).astype(BF16)
        for h in range(2):
            gather2[k, h] = []
        for d in (2, 1, 3):
            for h in range(2):
                b = axes(k, h)[1]
                mine = H.at[k, x, y, :, pl.ds(SPANS[h][0], SPANS[h][1] - SPANS[h][0])]
                gather2[k, h].append(send(mine, mine, on(b, d)))

    def f_gather(k, h):
        a, b, ia, ib = axes(k, h)
        for copy in gather2[k, h]:
            copy.wait_recv()
        low, top = piece(H, k, h, ia, 0), piece(H, k, h, ia, 1)
        gather1[k, h] = (send(low, low, on(a, 1)), send(top, top, on(a, -1)))
        forward[k, h] = [send(top, top, on(a, 1)), send(low, low, on(a, -1))]

    def f_forward(k, h, side):
        a, b, ia, ib = axes(k, h)
        gather1[k, h][side].wait_recv()
        block = piece(H, k, h, lax.rem(ia + (3, 1)[side], 4), side)
        forward[k, h].append(send(block, block, on(a, (1, -1)[side])))

    def f_project(k):
        for h in range(2):
            for copy in forward[k, h]:
                copy.wait_recv()
        full = H[k].reshape(256, COLS)
        mlp = dot(full[:, BACK:], WD[...], ((1,), (0,))).astype(BF16)
        grad = dot(full[:, :BACK], WJ[...], ((1,), (0,))).astype(BF16)
        for who in (1, 0):
            for p in range(4):
                at_row = 64 * p + 32 * who
                Q[k, who, p, :, :WID] = mlp[at_row : at_row + 32]
                Q[k, who, p, :, WID:] = grad[at_row : at_row + 32]
        swap[k] = send(Q.at[k, 1], E.at[k], at(dc=1))

    landings = []

    def hand_on(d, to, sign):
        n = len(landings)
        landings.append(d)
        k, p = SLOT[d]
        return n, send(S.at[k, p], LAND.at[n], at(dz=d - to))

    def f_pair(k):
        swap[k].wait_recv()
        S[k] = (Q[k, 0].astype(F32) + E[k].astype(F32)).astype(BF16)
        for d in CHUNKS[k]:
            sign = 1 if d > 0 else -1
            if abs(d) == 2:
                last.append(hand_on(d, 0, sign))
            elif d and d % 2 == 0:
                even[d] = hand_on(d, d - sign, sign)

    def f_odd(d):
        k, p = SLOT[d]
        sign = 1 if d > 0 else -1
        total = S[k, p].astype(F32)
        for table, other in ((even, d + sign), (odd, d + 2 * sign)):
            if other in table:
                n, copy = table[other]
                copy.wait_recv()
                total = total + LAND[n].astype(F32)
        S[k, p] = total.astype(BF16)
        if abs(d) == 1 or abs(d) in DIRECT:
            last.append(hand_on(d, 0, sign))
        else:
            odd[d] = hand_on(d, d - 2 * sign, sign)

    started = []

    def f_grads(k):
        full = H[k].reshape(256, COLS)
        both = X[k].reshape(256, 2 * WID)
        inv = full[:, 3 * HID : 3 * HID + 1].astype(F32) + full[:, 3 * HID + 1 : 3 * HID + 2].astype(F32)
        normed = (both[:, :WID].astype(F32) * inv * gain()).astype(BF16)
        joined = dot(full[:, :BACK], normed, ((0,), (0,)))
        down = dot(full[:, BACK:], both[:, WID:], ((0,), (0,)))[:HID]
        if started:
            joined_ref[...] += joined
            down_ref[...] += down
        else:
            joined_ref[...] = joined
            down_ref[...] = down
        started.append(k)

    steps = {
        "X": f_pass, "A": f_partial, "B": f_merge, "C": f_second, "D": f_act, "E": f_gather, "F": f_forward,
        "G": f_project, "I": f_pair, "J": f_odd, "R": f_grads,
    }
    f_pass(0)
    for copy in fetch[3:]:
        copy.wait()
    for line in SCHEDULE:
        for step in line.split():
            numbers = (int(step[1:]),) if step[0] in "XJ" else tuple(int(c) for c in step[1:])
            steps[step[0]](*numbers)

    k, p = SLOT[0]
    total = S[k, p].astype(F32)
    for n, copy in last:
        copy.wait_recv()
        total = total + LAND[n].astype(F32)
    acts_ref[...] = total.astype(BF16)
    for copy in pending:
        copy.wait_send()


def deliver(acts, joined, down, out_ref, ig_ref, gg_ref, gu_ref, gd_ref, sems):
    copies = [
        pltpu.make_async_copy(src, dst, sems.at[i])
        for i, (src, dst) in enumerate((
            (joined.at[pl.ds(0, HID)], gg_ref),
            (joined.at[pl.ds(HID, HID)], gu_ref),
            (down, gd_ref),
            (acts.at[:, pl.ds(0, WID)], out_ref),
            (acts.at[:, pl.ds(WID, WID)], ig_ref),
        ))
    ]
    for copy in copies:
        copy.start()
    for copy in copies:
        copy.wait()


COPIES = 15 + 16 + 36 * 4 + 4 + 15


def shards(mantissa, block_exponents, norm_gain, gate_weight, up_weight, down_weight, cotangent):
    vmem = pl.BlockSpec(memory_space=pltpu.VMEM)
    hbm = pl.BlockSpec(memory_space=pltpu.HBM)
    widths = [b - a for a, b in SPANS]
    acts, joined, down = pl.pallas_call(
        layer,
        out_shape=(
            jax.ShapeDtypeStruct((32, 2 * WID), BF16),
            jax.ShapeDtypeStruct((BACK, WID), F32),
            jax.ShapeDtypeStruct((HID, WID), F32),
        ),
        in_specs=[hbm, hbm, vmem, hbm, hbm, hbm, hbm],
        out_specs=[vmem] * 3,
        scratch_shapes=[
            pltpu.VMEM((32, WID), BF16),
            pltpu.VMEM((32, WID), jnp.int32),
            pltpu.VMEM((4, 4, 2, 32, 2 * WID), BF16),
            pltpu.VMEM((BACK, WID), BF16),
            pltpu.VMEM((512, WID), BF16),
            pltpu.VMEM((4, 4, 4, 16, COLS), BF16),
            pltpu.VMEM((4, 6, 2, 16, widths[0]), BF16),
            pltpu.VMEM((4, 6, 2, 16, widths[1]), BF16),
            pltpu.VMEM((4, 3, 16, widths[0]), BF16),
            pltpu.VMEM((4, 3, 16, widths[1]), BF16),
            pltpu.VMEM((4, 4, 4, 16, COLS), BF16),
            pltpu.VMEM((4, 2, 4, 32, 2 * WID), BF16),
            pltpu.VMEM((4, 4, 32, 2 * WID), BF16),
            pltpu.VMEM((4, 4, 32, 2 * WID), BF16),
            pltpu.VMEM((15, 32, 2 * WID), BF16),
            pltpu.SemaphoreType.DMA((COPIES,)),
            pltpu.SemaphoreType.DMA((COPIES,)),
            pltpu.SemaphoreType.DMA((6,)),
        ],
        compiler_params=pltpu.CompilerParams(collective_id=0, has_side_effects=True, vmem_limit_bytes=48 << 20),
        name="swiglu_layer",
    )(mantissa, block_exponents, norm_gain, gate_weight.T, up_weight.T, down_weight, cotangent)
    out, grad, gg, gu, gd = pl.pallas_call(
        deliver,
        out_shape=(
            jax.ShapeDtypeStruct((32, WID), BF16),
            jax.ShapeDtypeStruct((32, WID), BF16),
            jax.ShapeDtypeStruct((HID, WID), F32),
            jax.ShapeDtypeStruct((HID, WID), F32),
            jax.ShapeDtypeStruct((HID, WID), F32),
        ),
        in_specs=[vmem] * 3,
        out_specs=[hbm] * 5,
        scratch_shapes=[pltpu.SemaphoreType.DMA((5,))],
        compiler_params=pltpu.CompilerParams(vmem_limit_bytes=2 << 20),
        name="deliver",
    )(acts, joined, down)
    return out, grad, gg.T, gu.T, gd


def solution(mesh):
    in_specs = (
        P("tensor", "dp"),
        P("tensor", None),
        P("dp"),
        P("dp", "tensor"),
        P("dp", "tensor"),
        P("tensor", "dp"),
        P("tensor", "dp"),
    )
    out_specs = (
        P("tensor", "dp"),
        P("tensor", "dp"),
        P("dp", "tensor"),
        P("dp", "tensor"),
        P("tensor", "dp"),
    )
    return jax.shard_map(shards, mesh=mesh, in_specs=in_specs, out_specs=out_specs, check_vma=False)
```

time: 467 us -> 86.6 us (0.19)
  the two profiles are of different devices: /device:TPU:6 before, /device:TPU:8 now
where the time goes in v1:
time: 86.6 us; the launch traced here: 86.2 us
  Pallas kernels  79.9 us (92%)
  local copies, waits for them, and re-layouts  5.65 us (7%)
    pallas_call x1, Pallas kernels, shards(): pl.pallas_call(layer, out_shape=(jax.ShapeDtypeStruct((32, 2 * WID), BF16...  78.8 us
    unnamed x14, local copies, waits for them, and re-layouts  5.65 us

profile of v1, /device:TPU:8, one launch (start us, length us, event | category | flops | bytes accessed | tf_op | source)
XLA Modules:
  0.0 86.2 jit_solution(8737165553273996240)
XLA Ops:
  0.6 0.0 copy-start.6
  0.6 0.6 copy-done.6
  1.3 0.0 copy-start
  1.3 0.9 %copy-done = bf16[256,448]{0,1:T(8,128)(2,1)S(1)} copy-done((bf16[256,448]{0,1:T(8,128)(2,1)S(1)}, bf16[256,448]{0,1:T(8,128)(2,1)}, u32[]{:S(2)}) %copy-start) | copy-done | bytes 229400
  2.2 0.0 copy-start.1
  2.2 0.9 %copy-done.1 = bf16[256,448]{0,1:T(8,128)(2,1)S(1)} copy-done((bf16[256,448]{0,1:T(8,128)(2,1)S(1)}, bf16[256,448]{0,1:T(8,128)(2,1)}, u32[]{:S(2)}) %copy-start.1) | copy-done | bytes 229400
  3.2 0.0 copy-start.2
  3.2 0.9 %copy-done.2 = bf16[448,256]{1,0:T(8,128)(2,1)S(1)} copy-done((bf16[448,256]{1,0:T(8,128)(2,1)S(1)}, bf16[448,256]{1,0:T(8,128)(2,1)}, u32[]{:S(2)}) %copy-start.2) | copy-done | bytes 229400
  4.1 0.0 copy-start.3
  4.1 0.8 copy-done.3
  4.9 0.0 copy-start.4
  4.9 0.7 copy-done.4
  5.6 0.0 copy-start.5
  5.6 0.7 copy-done.5
  6.3 78.8 %swiglu_layer.1 = (bf16[32,512]{1,0:T(8,128)(2,1)S(1)}, f32[896,256]{1,0:T(8,128)S(1)}, f32[448,256]{1,0:T(8,128)S(1)}) custom-call(bf16[32,256]{1,0:T(8,128)(2,1)S(1)} %copy-done.4, s32[32,256]{1,0:T(8,128)S(1)} %copy-done.3, bf16[256]{0:T(256)(128)(2,1)S(1)} %copy-done.6, bf16[448,256]{1,0:T(8,128)(2,1)S(1)} %bitcast.4, bf16[448,256]{1,0:T(8,128)(2,1)S(1)} %bitcast.5, ...), custom_call_target="tpu_custom_call" | custom-call | tf_op jit(solution)/shard_map/swiglu_layer/pallas_call | solution.py:378
  85.1 1.1 %deliver.1 = (bf16[32,256]{1,0:T(8,128)(2,1)}, bf16[32,256]{1,0:T(8,128)(2,1)}, f32[448,256]{1,0:T(8,128)}, f32[448,256]{1,0:T(8,128)}, f32[448,256]{1,0:T(8,128)}) custom-call(bf16[32,512]{1,0:T(8,128)(2,1)S(1)} %get-tuple-element.13.acts, f32[896,256]{1,0:T(8,128)S(1)} %get-tuple-element.14.joined, f32[448,256]{1,0:T(8,128)S(1)} %get-tuple-element.15.down), custom_call_target="tpu_custom_call" | custom-call | tf_op jit(solution)/shard_map/deliver/pallas_call | solution.py:410
Async XLA Ops:
  0.6 0.7 copy-start.6
  1.3 0.9 %copy-start = (bf16[256,448]{0,1:T(8,128)(2,1)S(1)}, bf16[256,448]{0,1:T(8,128)(2,1)}, u32[]{:S(2)}) copy-start(bf16[256,448]{0,1:T(8,128)(2,1)} %param.10) | copy-start | bytes 688132
  2.2 0.9 %copy-start.1 = (bf16[256,448]{0,1:T(8,128)(2,1)S(1)}, bf16[256,448]{0,1:T(8,128)(2,1)}, u32[]{:S(2)}) copy-start(bf16[256,448]{0,1:T(8,128)(2,1)} %param.11) | copy-start | bytes 688132
  3.2 0.9 %copy-start.2 = (bf16[448,256]{1,0:T(8,128)(2,1)S(1)}, bf16[448,256]{1,0:T(8,128)(2,1)}, u32[]{:S(2)}) copy-start(bf16[448,256]{1,0:T(8,128)(2,1)} %wd_hbm.1) | copy-start | bytes 688132
  4.1 0.8 copy-start.3
  4.9 0.7 copy-start.4
  5.6 0.7 copy-start.5

commit v2 on v1

--- a/solution.py
+++ b/solution.py
@@ -23,26 +23,26 @@
 DIRECT = (5,)
 SCHEDULE = (
     "X-1 X1 X-2 X2",
-    "A0 X3 X-3 X-4",
-    "X4 A1 X5 X-5",
-    "B000 B001 B010 B011",
-    "X6 X-6 B100 B101",
-    "B110 B111 A2 X7",
-    "X-7 C01 C00 X8",
-    "C10 C11 A3 B200",
-    "B201 B210 B211 D0",
-    "D1 B300 B301 B310",
-    "B311 C21 C20 E00",
-    "E01 E11 E10 C30",
-    "C31 D2 F000 F001",
-    "F010 F011 F100 F101",
-    "F110 F111 D3 E20",
-    "E21 G0 R0 G1",
-    "R1 I0 E30 F200",
-    "F201 F210 F211 I1",
-    "E31 F300 F301 J3",
+    "A0 X-3 X3 X-4",
+    "X4 B000 B001 B010",
+    "B011 A1 X-5 X5",
+    "X-6 C00 X6 C01",
+    "B110 B111 B100 B101",
+    "A2 X-7 X7 X8",
+    "D0 C10 C11 A3",
+    "B210 B211 B200 B201",
+    "E00 E01 D1 B300",
+    "B301 B310 B311 C21",
+    "C20 F010 F011 F000",
+    "F001 E10 E11 C31",
+    "C30 D2 G0 R0",
+    "F100 F101 F110 F111",
+    "I0 D3 E20 E21",
+    "G1 R1 I1 E30",
+    "E31 F200 F201 F210",
+    "F211 J3 F300 F301",
     "F310 F311 G2 R2",
-    "I2 G3 J1 R3",
+    "J1 G3 R3 I2",
     "I3 J-7 J-3 J7",
     "J-5 J-1 J5",
 )
@@ -62,8 +62,8 @@
 
 def layer(
     m_hbm, e_hbm, g_ref, wg_hbm, wu_hbm, wd_hbm, c_hbm,
-    acts_ref, joined_ref, down_ref,
-    MV, EV, X, WJ, WD, PB, R1A, R1B, R2A, R2B, H, Q, E, S, LAND, ss, rs, ls,
+    acts_hbm, joined_hbm, down_hbm,
+    MV, EV, X, WJ, WD, PB, R1A, R1B, R2A, R2B, H, Q, E, S, LAND, joined_ref, down_ref, acts_ref, ss, rs, ls, ws,
 ):
     dp, tn = lax.axis_index("dp"), lax.axis_index("tensor")
     x, y = dp // NY, lax.rem(dp, NY)
@@ -312,7 +312,7 @@
         else:
             odd[d] = hand_on(d, d - 2 * sign, sign)
 
-    started = []
+    started, results = [], []
 
     def f_grads(k):
         full = H[k].reshape(256, COLS)
@@ -328,6 +328,11 @@
             joined_ref[...] = joined
             down_ref[...] = down
         started.append(k)
+        if len(started) == len(CHUNKS):
+            results.append(pltpu.make_async_copy(joined_ref, joined_hbm, ws.at[0]))
+            results.append(pltpu.make_async_copy(down_ref, down_hbm, ws.at[1]))
+            for copy in results:
+                copy.start()
 
     steps = {
         "X": f_pass, "A": f_partial, "B": f_merge, "C": f_second, "D": f_act, "E": f_gather, "F": f_forward,
@@ -347,24 +352,31 @@
         copy.wait_recv()
         total = total + LAND[n].astype(F32)
     acts_ref[...] = total.astype(BF16)
+    results.append(pltpu.make_async_copy(acts_ref, acts_hbm, ws.at[2]))
+    results[-1].start()
     for copy in pending:
         copy.wait_send()
-
-
-def deliver(acts, joined, down, out_ref, ig_ref, gg_ref, gu_ref, gd_ref, sems):
-    copies = [
-        pltpu.make_async_copy(src, dst, sems.at[i])
-        for i, (src, dst) in enumerate((
-            (joined.at[pl.ds(0, HID)], gg_ref),
-            (joined.at[pl.ds(HID, HID)], gu_ref),
-            (down, gd_ref),
-            (acts.at[:, pl.ds(0, WID)], out_ref),
-            (acts.at[:, pl.ds(WID, WID)], ig_ref),
-        ))
-    ]
-    for copy in copies:
+    for copy in results:
+        copy.wait()
+
+
+def deliver(acts, joined, down, out_ref, ig_ref, gg_ref, gu_ref, gd_ref, AV, JV, DV, rsem, wsem):
+    half = HID // 2
+    plan = [(acts, AV, (AV.at[:, pl.ds(0, WID)], out_ref), (AV.at[:, pl.ds(WID, WID)], ig_ref))]
+    for src, via, start, dst in ((joined, JV, 0, gg_ref), (joined, JV, HID, gu_ref), (down, DV, 0, gd_ref)):
+        for part in (0, half):
+            there = pl.ds(start + part, half)
+            plan.append((src.at[there], via.at[there], (via.at[there], dst.at[pl.ds(part, half)])))
+    reads = [pltpu.make_async_copy(entry[0], entry[1], rsem.at[i]) for i, entry in enumerate(plan)]
+    for copy in reads:
         copy.start()
-    for copy in copies:
+    writes = []
+    for copy, entry in zip(reads, plan):
+        copy.wait()
+        for src, dst in entry[2:]:
+            writes.append(pltpu.make_async_copy(src, dst, wsem.at[len(writes)]))
+            writes[-1].start()
+    for copy in writes:
         copy.wait()
 
 
@@ -383,7 +395,7 @@
             jax.ShapeDtypeStruct((HID, WID), F32),
         ),
         in_specs=[hbm, hbm, vmem, hbm, hbm, hbm, hbm],
-        out_specs=[vmem] * 3,
+        out_specs=[hbm] * 3,
         scratch_shapes=[
             pltpu.VMEM((32, WID), BF16),
             pltpu.VMEM((32, WID), jnp.int32),
@@ -400,11 +412,15 @@
             pltpu.VMEM((4, 4, 32, 2 * WID), BF16),
             pltpu.VMEM((4, 4, 32, 2 * WID), BF16),
             pltpu.VMEM((15, 32, 2 * WID), BF16),
+            pltpu.VMEM((BACK, WID), F32),
+            pltpu.VMEM((HID, WID), F32),
+            pltpu.VMEM((32, 2 * WID), BF16),
             pltpu.SemaphoreType.DMA((COPIES,)),
             pltpu.SemaphoreType.DMA((COPIES,)),
             pltpu.SemaphoreType.DMA((6,)),
+            pltpu.SemaphoreType.DMA((3,)),
         ],
-        compiler_params=pltpu.CompilerParams(collective_id=0, has_side_effects=True, vmem_limit_bytes=48 << 20),
+        compiler_params=pltpu.CompilerParams(collective_id=0, has_side_effects=True, vmem_limit_bytes=60 << 20),
         name="swiglu_layer",
     )(mantissa, block_exponents, norm_gain, gate_weight.T, up_weight.T, down_weight, cotangent)
     out, grad, gg, gu, gd = pl.pallas_call(
@@ -416,10 +432,16 @@
             jax.ShapeDtypeStruct((HID, WID), F32),
             jax.ShapeDtypeStruct((HID, WID), F32),
         ),
-        in_specs=[vmem] * 3,
+        in_specs=[hbm] * 3,
         out_specs=[hbm] * 5,
-        scratch_shapes=[pltpu.SemaphoreType.DMA((5,))],
-        compiler_params=pltpu.CompilerParams(vmem_limit_bytes=2 << 20),
+        scratch_shapes=[
+            pltpu.VMEM((32, 2 * WID), BF16),
+            pltpu.VMEM((BACK, WID), F32),
+            pltpu.VMEM((HID, WID), F32),
+            pltpu.SemaphoreType.DMA((7,)),
+            pltpu.SemaphoreType.DMA((8,)),
+        ],
+        compiler_params=pltpu.CompilerParams(vmem_limit_bytes=60 << 20),
         name="deliver",
     )(acts, joined, down)
     return out, grad, gg.T, gu.T, gd

time: 86.6 us -> 82.5 us (0.953)
  the two profiles are of different devices: /device:TPU:8 before, /device:TPU:6 now
where the time goes in v2:
time: 82.5 us; the launch traced here: 82.1 us
  Pallas kernels  81.4 us (99%)
    pallas_call x1, Pallas kernels, shards(): pl.pallas_call(layer, out_shape=(jax.ShapeDtypeStruct((32, 2 * WID), BF16...  79.2 us
    pallas_call x1, Pallas kernels, shards(): pl.pallas_call(deliver, out_shape=(jax.ShapeDtypeStruct((32, WID), BF16),...  2.27 us

profile of v2, /device:TPU:6, one launch (start us, length us, event | category | flops | bytes accessed | tf_op | source)
XLA Modules:
  0.0 82.1 jit_solution(18218555410203702572)
XLA Ops:
  0.6 79.2 %swiglu_layer.1 = (bf16[32,512]{1,0:T(8,128)(2,1)}, f32[896,256]{1,0:T(8,128)}, f32[448,256]{1,0:T(8,128)}) custom-call(bf16[32,256]{1,0:T(8,128)(2,1)} %m_hbm.1, s32[32,256]{1,0:T(8,128)} %e_hbm.1, bf16[256]{0:T(256)(128)(2,1)} %g_ref.1, bf16[448,256]{1,0:T(8,128)(2,1)} %bitcast.4, bf16[448,256]{1,0:T(8,128)(2,1)} %bitcast.5, bf16[448,256]{1,0:T(8,128)(2,1)} %wd_hbm.1, ...), custom_call_target="tpu_custom_call" | custom-call | tf_op jit(solution)/shard_map/swiglu_layer/pallas_call | solution.py:390
  79.8 2.3 %deliver.1 = (bf16[32,256]{1,0:T(8,128)(2,1)}, bf16[32,256]{1,0:T(8,128)(2,1)}, f32[448,256]{1,0:T(8,128)}, f32[448,256]{1,0:T(8,128)}, f32[448,256]{1,0:T(8,128)}) custom-call(bf16[32,512]{1,0:T(8,128)(2,1)} %get-tuple-element.13.acts, f32[896,256]{1,0:T(8,128)} %get-tuple-element.14.joined, f32[448,256]{1,0:T(8,128)} %get-tuple-element.15.down), custom_call_target="tpu_custom_call" | custom-call | tf_op jit(solution)/shard_map/deliver/pallas_call | solution.py:426

commit v3 on v1

--- a/solution.py
+++ b/solution.py
@@ -23,27 +23,27 @@
 DIRECT = (5,)
 SCHEDULE = (
     "X-1 X1 X-2 X2",
-    "A0 X3 X-3 X-4",
-    "X4 A1 X5 X-5",
-    "B000 B001 B010 B011",
-    "X6 X-6 B100 B101",
-    "B110 B111 A2 X7",
-    "X-7 C01 C00 X8",
-    "C10 C11 A3 B200",
-    "B201 B210 B211 D0",
-    "D1 B300 B301 B310",
-    "B311 C21 C20 E00",
-    "E01 E11 E10 C30",
-    "C31 D2 F000 F001",
-    "F010 F011 F100 F101",
-    "F110 F111 D3 E20",
-    "E21 G0 R0 G1",
-    "R1 I0 E30 F200",
-    "F201 F210 F211 I1",
-    "E31 F300 F301 J3",
-    "F310 F311 G2 R2",
-    "I2 G3 J1 R3",
-    "I3 J-7 J-3 J7",
+    "A0 X-3 X3 X-4",
+    "X4 B000 B001 A1",
+    "B010 X5 X-5 B011",
+    "X-6 X6 C00 B100",
+    "B101 A2 X7 B110",
+    "X-7 B111 C01 X8",
+    "A3 C10 B200 B201",
+    "B210 B211 C11 D0",
+    "B300 B301 B310 B311",
+    "C21 D1 C20 E00",
+    "C30 E01 C31 E11",
+    "D2 E10 F010 F011",
+    "F000 F001 D3 F110",
+    "F111 E20 F100 F101",
+    "E21 G0 R0 E30",
+    "E31 G1 I0 R1",
+    "F200 F201 F210 F211",
+    "I1 F310 F311 F300",
+    "F301 G2 J3 R2",
+    "G3 R3 I2 I3",
+    "J-7 J1 J-3 J7",
     "J-5 J-1 J5",
 )
 
@@ -61,9 +61,9 @@
 
 
 def layer(
-    m_hbm, e_hbm, g_ref, wg_hbm, wu_hbm, wd_hbm, c_hbm,
+    m_hbm, e_hbm, g_hbm, wg_hbm, wu_hbm, wd_hbm, c_hbm,
     acts_ref, joined_ref, down_ref,
-    MV, EV, X, WJ, WD, PB, R1A, R1B, R2A, R2B, H, Q, E, S, LAND, ss, rs, ls,
+    MV, EV, g_ref, X, WJ, WD, PB, R1A, R1B, R2A, R2B, H, Q, E, S, LAND, ss, rs, ls,
 ):
     dp, tn = lax.axis_index("dp"), lax.axis_index("tensor")
     x, y = dp // NY, lax.rem(dp, NY)
@@ -107,6 +107,7 @@
             (wg_hbm, WJ.at[pl.ds(0, HID)]),
             (wu_hbm, WJ.at[pl.ds(HID, HID)]),
             (wd_hbm, WD.at[pl.ds(0, HID)]),
+            (g_hbm, g_ref),
         ))
     ]
     for copy in fetch:
@@ -375,6 +376,8 @@
     vmem = pl.BlockSpec(memory_space=pltpu.VMEM)
     hbm = pl.BlockSpec(memory_space=pltpu.HBM)
     widths = [b - a for a, b in SPANS]
+    here = (mantissa, block_exponents, norm_gain, gate_weight.T, up_weight.T, down_weight, cotangent)
+    here = [pltpu.with_memory_space_constraint(array, pltpu.HBM) for array in here]
     acts, joined, down = pl.pallas_call(
         layer,
         out_shape=(
@@ -382,11 +385,12 @@
             jax.ShapeDtypeStruct((BACK, WID), F32),
             jax.ShapeDtypeStruct((HID, WID), F32),
         ),
-        in_specs=[hbm, hbm, vmem, hbm, hbm, hbm, hbm],
+        in_specs=[hbm] * 7,
         out_specs=[vmem] * 3,
         scratch_shapes=[
             pltpu.VMEM((32, WID), BF16),
             pltpu.VMEM((32, WID), jnp.int32),
+            pltpu.VMEM((WID,), BF16),
             pltpu.VMEM((4, 4, 2, 32, 2 * WID), BF16),
             pltpu.VMEM((BACK, WID), BF16),
             pltpu.VMEM((512, WID), BF16),
@@ -402,11 +406,11 @@
             pltpu.VMEM((15, 32, 2 * WID), BF16),
             pltpu.SemaphoreType.DMA((COPIES,)),
             pltpu.SemaphoreType.DMA((COPIES,)),
-            pltpu.SemaphoreType.DMA((6,)),
+            pltpu.SemaphoreType.DMA((7,)),
         ],
         compiler_params=pltpu.CompilerParams(collective_id=0, has_side_effects=True, vmem_limit_bytes=48 << 20),
         name="swiglu_layer",
-    )(mantissa, block_exponents, norm_gain, gate_weight.T, up_weight.T, down_weight, cotangent)
+    )(*here)
     out, grad, gg, gu, gd = pl.pallas_call(
         deliver,
         out_shape=(

time: 86.6 us -> 79.5 us (0.918)
  the two profiles are of different devices: /device:TPU:8 before, /device:TPU:6 now
where the time goes in v3:
time: 79.5 us; the launch traced here: 78.9 us
  Pallas kernels  78.2 us (98%)
    pallas_call x1, Pallas kernels, shards(): pl.pallas_call(layer, out_shape=(jax.ShapeDtypeStruct((32, 2 * WID), BF16...  77.1 us

profile of v3, /device:TPU:6, one launch (start us, length us, event | category | flops | bytes accessed | tf_op | source)
XLA Modules:
  0.0 78.9 jit_solution(10481738653949795174)
XLA Ops:
  0.6 77.1 %swiglu_layer.1 = (bf16[32,512]{1,0:T(8,128)(2,1)S(1)}, f32[896,256]{1,0:T(8,128)S(1)}, f32[448,256]{1,0:T(8,128)S(1)}) custom-call(bf16[32,256]{1,0:T(8,128)(2,1)} %m_hbm.1, s32[32,256]{1,0:T(8,128)} %e_hbm.1, bf16[256]{0:T(256)(128)(2,1)} %g_hbm.1, bf16[448,256]{1,0:T(8,128)(2,1)} %bitcast.4, bf16[448,256]{1,0:T(8,128)(2,1)} %bitcast.5, ...), custom_call_target="tpu_custom_call" | custom-call | tf_op jit(solution)/shard_map/swiglu_layer/pallas_call | solution.py:381
  77.7 1.1 %deliver.1 = (bf16[32,256]{1,0:T(8,128)(2,1)}, bf16[32,256]{1,0:T(8,128)(2,1)}, f32[448,256]{1,0:T(8,128)}, f32[448,256]{1,0:T(8,128)}, f32[448,256]{1,0:T(8,128)}) custom-call(bf16[32,512]{1,0:T(8,128)(2,1)S(1)} %get-tuple-element.13.acts, f32[896,256]{1,0:T(8,128)S(1)} %get-tuple-element.14.joined, f32[448,256]{1,0:T(8,128)S(1)} %get-tuple-element.15.down), custom_call_target="tpu_custom_call" | custom-call | tf_op jit(solution)/shard_map/deliver/pallas_call | solution.py:414

commit v4 on v3

--- a/solution.py
+++ b/solution.py
@@ -16,7 +16,7 @@
 WID = 256
 COLS = 1408
 BACK = 2 * HID
-SPANS = ((0, 640), (640, 1408))
+SPANS = ((0, 768), (768, 1408))
 
 CHUNKS = ((0, 1, -1, 2), (-2, 3, -3, 4), (-4, 5, -5, 6), (-6, 7, -7, 8))
 SLOT = {d: (k, p) for k, ds in enumerate(CHUNKS) for p, d in enumerate(ds)}
@@ -24,27 +24,27 @@
 SCHEDULE = (
     "X-1 X1 X-2 X2",
     "A0 X-3 X3 X-4",
-    "X4 B000 B001 A1",
-    "B010 X5 X-5 B011",
-    "X-6 X6 C00 B100",
-    "B101 A2 X7 B110",
-    "X-7 B111 C01 X8",
-    "A3 C10 B200 B201",
-    "B210 B211 C11 D0",
-    "B300 B301 B310 B311",
-    "C21 D1 C20 E00",
-    "C30 E01 C31 E11",
-    "D2 E10 F010 F011",
-    "F000 F001 D3 F110",
-    "F111 E20 F100 F101",
-    "E21 G0 R0 E30",
-    "E31 G1 I0 R1",
-    "F200 F201 F210 F211",
-    "I1 F310 F311 F300",
-    "F301 G2 J3 R2",
-    "G3 R3 I2 I3",
-    "J-7 J1 J-3 J7",
-    "J-5 J-1 J5",
+    "X4 B000 B001 B010",
+    "B011 A1 X-5 X5",
+    "X-6 X6 C00 C01",
+    "A2 B110 B111 B100",
+    "B101 X-7 X7 X8",
+    "D0 A3 B210 B200",
+    "B201 B211 C10 C11",
+    "E00 E01 B300 B301",
+    "B310 B311 C21 C20",
+    "D1 F010 F011 F000",
+    "F001 C30 C31 D2",
+    "E11 E10 G0 D3",
+    "I0 E21 E20 F100",
+    "F101 F110 F111 E31",
+    "E30 F210 F211 F200",
+    "F201 G1 F300 F301",
+    "F310 F311 I1 G2",
+    "G3 I2 J3 I3",
+    "J-7 J-3 J1 J7",
+    "J-5 J-1 J5 R0",
+    "R1 R2 R3",
 )
 
 
@@ -137,7 +137,7 @@
     def f_pass(d):
         if d != 0:
             ring[d].wait_recv()
-        for step in (-1, 1, -2, 2) if d == 0 else (-2,) if d < 0 else (2,):
+        for step in (2, -1, 1, -2) if d == 0 else (-2,) if d < 0 else (2,):
             if -8 < d + step < 9:
                 ring[d + step] = send(xat(d, 0), xat(d + step, 0), at(dz=-step))
         twin[d] = send(xat(d, 0), xat(d, 1), at(dc=1))
@@ -167,22 +167,25 @@
             twin[d].wait_recv()
         both = X[k].reshape(256, 2 * WID)
         values = both[:, :WID].astype(F32)
-        squares = jnp.sum(values * values, axis=1, keepdims=True)
         scaled = (values * gain()).astype(BF16)
         joined = dot(scaled, WJ[...], ((1,), (1,)))
         PB[k, :, :, :, :BACK] = joined.astype(BF16).reshape(4, 4, 16, BACK)
-        back = dot(both[:, WID:], WD[...], ((1,), (1,)))
-        lane = lax.broadcasted_iota(jnp.int32, back.shape, 1)
-        high = squares.astype(BF16).astype(F32)
-        back = jnp.where(lane == HID, high, jnp.where(lane == HID + 1, squares - high, back))
-        PB[k, :, :, :, BACK:] = back.astype(BF16).reshape(4, 4, 16, 512)
-        for h in range(2):
+        def send_far(h):
             a, b, ia, ib = axes(k, h)
             far = lax.rem(ia + 2, 4)
             first[k, h] = (
                 send(piece(PB, k, h, far, 0), R1[h].at[k, 0], on(a, 1)),
                 send(piece(PB, k, h, far, 1), R1[h].at[k, 1], on(a, -1)),
             )
+
+        send_far(0)
+        back = dot(both[:, WID:], WD[...], ((1,), (1,)))
+        lane = lax.broadcasted_iota(jnp.int32, back.shape, 1)
+        squares = jnp.sum(values * values, axis=1, keepdims=True)
+        high = squares.astype(BF16).astype(F32)
+        back = jnp.where(lane == HID, high, jnp.where(lane == HID + 1, squares - high, back))
+        PB[k, :, :, :, BACK:] = back.astype(BF16).reshape(4, 4, 16, 512)
+        send_far(1)
         for h in range(2):
             a, b, ia, ib = axes(k, h)
             right, left = lax.rem(ia + 1, 4), lax.rem(ia + 3, 4)

time: 79.5 us -> 79 us (level)
  Pallas kernels: 78.2 us -> 77.2 us
    pallas_call x1, Pallas kernels: 77.1 us -> 76.1 us  [shards(): pl.pallas_call(layer, out_shape=(jax.ShapeDtypeStruct((32, 2 * WID), BF16...]
where the time goes in v4:
time: 79 us; the launch traced here: 77.8 us
  Pallas kernels  77.2 us (98%)
    pallas_call x1, Pallas kernels, shards(): pl.pallas_call(layer, out_shape=(jax.ShapeDtypeStruct((32, 2 * WID), BF16...  76.1 us

profile of v4, /device:TPU:6, one launch (start us, length us, event | category | flops | bytes accessed | tf_op | source)
XLA Modules:
  0.0 77.8 jit_solution(4210268139172026764)
XLA Ops:
  0.6 76.1 %swiglu_layer.1 = (bf16[32,512]{1,0:T(8,128)(2,1)S(1)}, f32[896,256]{1,0:T(8,128)S(1)}, f32[448,256]{1,0:T(8,128)S(1)}) custom-call(bf16[32,256]{1,0:T(8,128)(2,1)} %m_hbm.1, s32[32,256]{1,0:T(8,128)} %e_hbm.1, bf16[256]{0:T(256)(128)(2,1)} %g_hbm.1, bf16[448,256]{1,0:T(8,128)(2,1)} %bitcast.4, bf16[448,256]{1,0:T(8,128)(2,1)} %bitcast.5, ...), custom_call_target="tpu_custom_call" | custom-call | tf_op jit(solution)/shard_map/swiglu_layer/pallas_call | solution.py:384
  76.7 1.1 %deliver.1 = (bf16[32,256]{1,0:T(8,128)(2,1)}, bf16[32,256]{1,0:T(8,128)(2,1)}, f32[448,256]{1,0:T(8,128)}, f32[448,256]{1,0:T(8,128)}, f32[448,256]{1,0:T(8,128)}) custom-call(bf16[32,512]{1,0:T(8,128)(2,1)S(1)} %get-tuple-element.13.acts, f32[896,256]{1,0:T(8,128)S(1)} %get-tuple-element.14.joined, f32[448,256]{1,0:T(8,128)S(1)} %get-tuple-element.15.down), custom_call_target="tpu_custom_call" | custom-call | tf_op jit(solution)/shard_map/deliver/pallas_call | solution.py:417

commit v5 on v3

--- a/solution.py
+++ b/solution.py
@@ -167,22 +167,25 @@
             twin[d].wait_recv()
         both = X[k].reshape(256, 2 * WID)
         values = both[:, :WID].astype(F32)
-        squares = jnp.sum(values * values, axis=1, keepdims=True)
         scaled = (values * gain()).astype(BF16)
         joined = dot(scaled, WJ[...], ((1,), (1,)))
         PB[k, :, :, :, :BACK] = joined.astype(BF16).reshape(4, 4, 16, BACK)
-        back = dot(both[:, WID:], WD[...], ((1,), (1,)))
-        lane = lax.broadcasted_iota(jnp.int32, back.shape, 1)
-        high = squares.astype(BF16).astype(F32)
-        back = jnp.where(lane == HID, high, jnp.where(lane == HID + 1, squares - high, back))
-        PB[k, :, :, :, BACK:] = back.astype(BF16).reshape(4, 4, 16, 512)
-        for h in range(2):
+        def send_far(h):
             a, b, ia, ib = axes(k, h)
             far = lax.rem(ia + 2, 4)
             first[k, h] = (
                 send(piece(PB, k, h, far, 0), R1[h].at[k, 0], on(a, 1)),
                 send(piece(PB, k, h, far, 1), R1[h].at[k, 1], on(a, -1)),
             )
+
+        send_far(0)
+        back = dot(both[:, WID:], WD[...], ((1,), (1,)))
+        lane = lax.broadcasted_iota(jnp.int32, back.shape, 1)
+        squares = jnp.sum(values * values, axis=1, keepdims=True)
+        high = squares.astype(BF16).astype(F32)
+        back = jnp.where(lane == HID, high, jnp.where(lane == HID + 1, squares - high, back))
+        PB[k, :, :, :, BACK:] = back.astype(BF16).reshape(4, 4, 16, 512)
+        send_far(1)
         for h in range(2):
             a, b, ia, ib = axes(k, h)
             right, left = lax.rem(ia + 1, 4), lax.rem(ia + 3, 4)

time: 79.5 us -> 78.9 us (level)
  no operation moved by 1% of the time
where the time goes in v5:
time: 78.9 us; the launch traced here: 78.6 us
  Pallas kernels  78 us (99%)
    pallas_call x1, Pallas kernels, shards(): pl.pallas_call(layer, out_shape=(jax.ShapeDtypeStruct((32, 2 * WID), BF16...  76.9 us

profile of v5, /device:TPU:6, one launch (start us, length us, event | category | flops | bytes accessed | tf_op | source)
XLA Modules:
  0.0 78.6 jit_solution(10546660123651273009)
XLA Ops:
  0.6 76.9 %swiglu_layer.1 = (bf16[32,512]{1,0:T(8,128)(2,1)S(1)}, f32[896,256]{1,0:T(8,128)S(1)}, f32[448,256]{1,0:T(8,128)S(1)}) custom-call(bf16[32,256]{1,0:T(8,128)(2,1)} %m_hbm.1, s32[32,256]{1,0:T(8,128)} %e_hbm.1, bf16[256]{0:T(256)(128)(2,1)} %g_hbm.1, bf16[448,256]{1,0:T(8,128)(2,1)} %bitcast.4, bf16[448,256]{1,0:T(8,128)(2,1)} %bitcast.5, ...), custom_call_target="tpu_custom_call" | custom-call | tf_op jit(solution)/shard_map/swiglu_layer/pallas_call | solution.py:384
  77.5 1.1 %deliver.1 = (bf16[32,256]{1,0:T(8,128)(2,1)}, bf16[32,256]{1,0:T(8,128)(2,1)}, f32[448,256]{1,0:T(8,128)}, f32[448,256]{1,0:T(8,128)}, f32[448,256]{1,0:T(8,128)}) custom-call(bf16[32,512]{1,0:T(8,128)(2,1)S(1)} %get-tuple-element.13.acts, f32[896,256]{1,0:T(8,128)S(1)} %get-tuple-element.14.joined, f32[448,256]{1,0:T(8,128)S(1)} %get-tuple-element.15.down), custom_call_target="tpu_custom_call" | custom-call | tf_op jit(solution)/shard_map/deliver/pallas_call | solution.py:417
